TPU v7x, 32 devices: a whole 2x2x4 slice. The times are simulated.
32 devices in a mesh: wide: 8 (over z, x), narrow: 4 (over y, core).
Axes of the slice: x: 2, y: 2, z: 4, core: 2. Of those that a mesh axis runs over, the one named last changes fastest.
Arguments:
- tokens: bfloat16 [2, 32768, 512], P(None, ('wide', 'narrow')), may hold values from -6 to 6
- out_grad: bfloat16 [2, 32768, 512], P(None, ('wide', 'narrow')), may hold values from -6 to 6
- long_count: int32 [2, 32], P(None, ('wide', 'narrow')), may hold values from 0 to 1
- params: float32 [3676160], P(('wide', 'narrow')), may hold values from -3 to 3, as said below
Outputs:
- outputs: bfloat16 [2, 32768, 512], P(None, ('wide', 'narrow'))
- input_grad: bfloat16 [2, 32768, 512], P(None, ('wide', 'narrow'))
- param_grad: float32 [3676160], P(('wide', 'narrow'))
Inputs may be any that keep to these rules, and one draw needn't show every extreme that they name: `params`: the packed parameters, laid out as the first step states.
All inputs are finite; a program needn't handle non-finite values.
Results may differ from a plain program's by a relative error of at most 0.011.
Values may be sent and summed in bfloat16 or wider, within the bound.
No kernel may reach another device: no remote copies, remote signals or barrier semaphores. Data moves between devices by JAX's collectives and lax.ppermute only.
A program may use at most 192 MiB of HBM per device.

v0:
```python
import math

import jax
import jax.numpy as jnp
from jax import lax
from jax.sharding import PartitionSpec as P

D = 512
FF = 2048
HEADS = 8
HD = 64
SHORT = 512
LONG = 1024


layer_eps = 1e-05
masked_value = -1000000000.0


def product(left, right):
    return jnp.dot(left, right, preferred_element_type=jnp.float32)


def rows_inner(left, right):
    return lax.dot_general(
        left, right, (((0,), (0,)), ((), ())), preferred_element_type=jnp.float32
    )


def times_trans(left, right):
    return lax.dot_general(
        left, right, (((1,), (1,)), ((), ())), preferred_element_type=jnp.float32
    )


def unpack(buffer):
    square = D * D
    matrices = tuple(
        (buffer[position * square : (position + 1) * square].reshape(D, D) for position in range(6))
    )
    offset = 6 * square
    weight_in = buffer[offset : offset + D * FF].reshape(D, FF)
    offset = offset + D * FF
    weight_out = buffer[offset : offset + FF * D].reshape(FF, D)
    offset = offset + FF * D
    vectors = tuple(
        (buffer[offset + position * D : offset + (position + 1) * D] for position in range(8))
    )
    offset = offset + 8 * D
    bias_in = buffer[offset : offset + FF]
    return matrices + (weight_in, weight_out) + vectors + (bias_in,)


def layer_stats(values):
    average = jnp.mean(values, -1, keepdims=True)
    centred = values - average
    variance = jnp.mean(centred * centred, -1, keepdims=True)
    inv_std = lax.rsqrt(variance + layer_eps)
    return (centred * inv_std, inv_std)


def norm_back(grad_hat, normed, inv_std):
    return inv_std * (
        grad_hat
        - jnp.mean(grad_hat, -1, keepdims=True)
        - normed * jnp.mean(grad_hat * normed, -1, keepdims=True)
    )


def window_mask(length, is_long):
    row_ids = lax.broadcasted_iota(jnp.int32, (length, length), 0)
    col_ids = lax.broadcasted_iota(jnp.int32, (length, length), 1)
    same_seq = is_long | (row_ids // SHORT == col_ids // SHORT)
    return same_seq & (row_ids >= col_ids)


def head_scores(query_rows, key_rows, is_long):
    factor = 1.0 / math.sqrt(query_rows.shape[1])
    scores = times_trans(query_rows, key_rows) * factor
    return jnp.where(window_mask(query_rows.shape[0], is_long), scores, masked_value)


def split_heads(rows_array):
    return rows_array.reshape(rows_array.shape[0], HEADS, HD).transpose(1, 0, 2)


def to_windows(rows_array):
    return rows_array.reshape((rows_array.shape[0] // LONG, LONG) + rows_array.shape[1:])


def heads_to_rows(stacked):
    return stacked.transpose(0, 2, 1, 3).reshape(stacked.shape[0] * LONG, HEADS * HD)


def window_forward(bundle):
    query_rows, key_rows, value_rows, is_long = bundle

    def head_forward(members):
        query_head, key_head, value_head = members
        scores = head_scores(query_head, key_head, is_long)
        largest = jnp.max(scores, -1, keepdims=True)
        shifted = jnp.exp(scores - largest)
        sum_exp = jnp.sum(shifted, -1, keepdims=True)
        soft_probs = (shifted / sum_exp).astype(jnp.bfloat16)
        output = product(soft_probs, value_head).astype(jnp.bfloat16)
        return (output, (largest + jnp.log(sum_exp))[:, 0])

    return lax.map(
        head_forward, (split_heads(query_rows), split_heads(key_rows), split_heads(value_rows))
    )


def window_backward(bundle):
    query_rows, key_rows, value_rows, grad_out, logsum, is_long = bundle

    def head_backward(members):
        query_head, key_head, value_head, grad_head, logsum_head = members
        factor = 1.0 / math.sqrt(query_head.shape[1])
        soft = jnp.exp(head_scores(query_head, key_head, is_long) - logsum_head[:, None])
        soft_probs = soft.astype(jnp.bfloat16)
        grad_probs = times_trans(grad_head, value_head)
        grad_scores = (soft * (grad_probs - jnp.sum(grad_probs * soft, -1, keepdims=True))).astype(
            jnp.bfloat16
        )
        grad_query = (product(grad_scores, key_head) * factor).astype(jnp.bfloat16)
        grad_key = (rows_inner(grad_scores, query_head) * factor).astype(jnp.bfloat16)
        grad_value = rows_inner(soft_probs, grad_head).astype(jnp.bfloat16)
        return (grad_query, grad_key, grad_value)

    return lax.map(
        head_backward,
        (
            split_heads(query_rows),
            split_heads(key_rows),
            split_heads(value_rows),
            split_heads(grad_out),
            logsum,
        ),
    )


def attend(query_rows, key_rows, value_rows, long_seqs):
    is_long = jnp.arange(query_rows.shape[0] // LONG) < long_seqs
    output, logsum = lax.map(
        window_forward,
        (to_windows(query_rows), to_windows(key_rows), to_windows(value_rows), is_long),
    )
    return (heads_to_rows(output), logsum)


def attend_back(query_rows, key_rows, value_rows, grad_out, logsum, long_seqs):
    is_long = jnp.arange(query_rows.shape[0] // LONG) < long_seqs
    results = lax.map(
        window_backward,
        (
            to_windows(query_rows),
            to_windows(key_rows),
            to_windows(value_rows),
            to_windows(grad_out),
            logsum,
            is_long,
        ),
    )
    return tuple((heads_to_rows(member) for member in results))


def split_weights(weights):
    matrices = weights[:8]
    vectors = tuple((vector.astype(jnp.float32) for vector in weights[8:]))
    return (matrices, vectors)


def forward_pass(weights, inputs, long_seqs):
    matrices, vectors = split_weights(weights)
    w_query, w_key, w_value, w_out, gate_attn, gate_ffn, weight_in, weight_out = matrices
    gain_a, shift_a, bias_out, bias_gate_a, gain_f, shift_f, bias_down, bias_gate_f, bias_in = (
        vectors
    )
    normed_a, inv_std_a = layer_stats(inputs)
    hidden_a = (normed_a * gain_a + shift_a).astype(jnp.bfloat16)
    query_rows = product(hidden_a, w_query).astype(jnp.bfloat16)
    key_rows = product(hidden_a, w_key).astype(jnp.bfloat16)
    value_rows = product(hidden_a, w_value).astype(jnp.bfloat16)
    attended, logsum = attend(query_rows, key_rows, value_rows, long_seqs)
    branch_a = product(attended, w_out) + bias_out
    gate_a = jax.nn.sigmoid(product(hidden_a, gate_attn) + bias_gate_a)
    middle = inputs + gate_a * branch_a
    normed_f, inv_std_f = layer_stats(middle)
    hidden_f = (normed_f * gain_f + shift_f).astype(jnp.bfloat16)
    pre_active = product(hidden_f, weight_in) + bias_in
    active = jax.nn.gelu(pre_active).astype(jnp.bfloat16)
    branch_f = product(active, weight_out) + bias_down
    gate_f = jax.nn.sigmoid(product(hidden_f, gate_ffn) + bias_gate_f)
    result = middle + gate_f * branch_f
    return {
        "normed_a": normed_a,
        "inv_std_a": inv_std_a,
        "hidden_a": hidden_a,
        "query_rows": query_rows,
        "key_rows": key_rows,
        "value_rows": value_rows,
        "attended": attended,
        "logsum": logsum,
        "branch_a": branch_a,
        "gate_a": gate_a,
        "normed_f": normed_f,
        "inv_std_f": inv_std_f,
        "hidden_f": hidden_f,
        "pre_active": pre_active,
        "active": active,
        "branch_f": branch_f,
        "gate_f": gate_f,
        "result": result,
    }


def backward_pass(weights, stored, grad_rows, long_seqs):
    matrices, vectors = split_weights(weights)
    w_query, w_key, w_value, w_out, gate_attn, gate_ffn, weight_in, weight_out = matrices
    gain_a, shift_a, bias_out, bias_gate_a, gain_f, shift_f, bias_down, bias_gate_f, bias_in = (
        vectors
    )
    gate_f = stored["gate_f"]
    grad_branch_f = (grad_rows * gate_f).astype(jnp.bfloat16)
    grad_zf = (grad_rows * stored["branch_f"] * gate_f * (1.0 - gate_f)).astype(jnp.bfloat16)
    d_weight_out = rows_inner(stored["active"], grad_branch_f)
    d_bias_down = jnp.sum(grad_branch_f.astype(jnp.float32), 0)
    grad_active = times_trans(grad_branch_f, weight_out)
    unused, gelu_back = jax.vjp(jax.nn.gelu, stored["pre_active"])
    grad_pre = gelu_back(grad_active)[0].astype(jnp.bfloat16)
    d_weight_in = rows_inner(stored["hidden_f"], grad_pre)
    d_bias_in = jnp.sum(grad_pre.astype(jnp.float32), 0)
    d_gate_ffn = rows_inner(stored["hidden_f"], grad_zf)
    d_bias_gate_f = jnp.sum(grad_zf.astype(jnp.float32), 0)
    grad_hidden_f = times_trans(grad_pre, weight_in) + times_trans(grad_zf, gate_ffn)
    d_gain_f = jnp.sum(grad_hidden_f * stored["normed_f"], 0)
    d_shift_f = jnp.sum(grad_hidden_f, 0)
    grad_middle = grad_rows + norm_back(
        grad_hidden_f * gain_f, stored["normed_f"], stored["inv_std_f"]
    )
    gate_a = stored["gate_a"]
    grad_branch_a = (grad_middle * gate_a).astype(jnp.bfloat16)
    grad_za = (grad_middle * stored["branch_a"] * gate_a * (1.0 - gate_a)).astype(jnp.bfloat16)
    d_w_out = rows_inner(stored["attended"], grad_branch_a)
    d_bias_out = jnp.sum(grad_branch_a.astype(jnp.float32), 0)
    d_gate_attn = rows_inner(stored["hidden_a"], grad_za)
    d_bias_gate_a = jnp.sum(grad_za.astype(jnp.float32), 0)
    grad_attended = times_trans(grad_branch_a, w_out).astype(jnp.bfloat16)
    grad_query, grad_key, grad_value = attend_back(
        stored["query_rows"],
        stored["key_rows"],
        stored["value_rows"],
        grad_attended,
        stored["logsum"],
        long_seqs,
    )
    hidden_a = stored["hidden_a"]
    d_query = rows_inner(hidden_a, grad_query)
    d_key = rows_inner(hidden_a, grad_key)
    d_value = rows_inner(hidden_a, grad_value)
    grad_hidden_a = (
        times_trans(grad_query, w_query)
        + times_trans(grad_key, w_key)
        + times_trans(grad_value, w_value)
        + times_trans(grad_za, gate_attn)
    )
    d_gain_a = jnp.sum(grad_hidden_a * stored["normed_a"], 0)
    d_shift_a = jnp.sum(grad_hidden_a, 0)
    grad_inputs = grad_middle + norm_back(
        grad_hidden_a * gain_a, stored["normed_a"], stored["inv_std_a"]
    )
    flat_grad = jnp.concatenate(
        [
            member.ravel()
            for member in (
                d_query,
                d_key,
                d_value,
                d_w_out,
                d_gate_attn,
                d_gate_ffn,
                d_weight_in,
                d_weight_out,
                d_gain_a,
                d_shift_a,
                d_bias_out,
                d_bias_gate_a,
                d_gain_f,
                d_shift_f,
                d_bias_down,
                d_bias_gate_f,
                d_bias_in,
            )
        ]
    )
    return (flat_grad, grad_inputs)


def on_device(tokens, out_grad, long_count, params):
    gathered = lax.all_gather(params.astype(jnp.bfloat16), ("wide", "narrow"), axis=0, tiled=True)
    weights = unpack(gathered)
    sub_total = tokens.shape[0]
    kept = []
    for sub_index in range(sub_total):
        kept.append(
            forward_pass(weights, tokens[sub_index].astype(jnp.float32), long_count[sub_index, 0])
        )
    outputs = jnp.stack([stored["result"] for stored in kept]).astype(jnp.bfloat16)
    back_buffer = lax.all_gather(
        params.astype(jnp.bfloat16), ("wide", "narrow"), axis=0, tiled=True
    )
    back_weights = unpack(back_buffer)
    running = None
    input_rows = [None] * sub_total
    for sub_index in reversed(range(sub_total)):
        flat_grad, grad_inputs = backward_pass(
            back_weights,
            kept[sub_index],
            out_grad[sub_index].astype(jnp.float32),
            long_count[sub_index, 0],
        )
        input_rows[sub_index] = grad_inputs
        running = flat_grad if running is None else running + flat_grad
    param_grad = lax.psum_scatter(running, ("wide", "narrow"), scatter_dimension=0, tiled=True)
    input_grad = jnp.stack(input_rows).astype(jnp.bfloat16)
    return (outputs, input_grad, param_grad)


def solution(mesh):
    return jax.shard_map(
        on_device,
        mesh=mesh,
        in_specs=(
            P(None, ("wide", "narrow"), None),
            P(None, ("wide", "narrow"), None),
            P(None, ("wide", "narrow")),
            P(("wide", "narrow")),
        ),
        out_specs=(
            P(None, ("wide", "narrow"), None),
            P(None, ("wide", "narrow"), None),
            P(("wide", "narrow")),
        ),
        check_vma=False,
    )
```

profile of v0, /device:TPU:0, one launch (start us, length us, event | category | flops | bytes accessed | tf_op | source)
XLA Modules:
  0.0 1041.7 jit_solution(1891951934400876862)
XLA Ops:
  11.6 4.7 dynamic-update-slice
  20.2 167.3 %all-reduce.5.cloned.1.call-done = bf16[3676160]{0:T(1024)(128)(2,1)} async-done(((bf16[3676160]{0:T(1024)(128)(2,1)}), bf16[3676160]{0:T(1024)(128)(2,1)}) %all-reduce.5.cloned.1.call-update) | async-done | bytes 7352336
  214.5 46.3 %while.104 = (s32[]{:T(128)}, bf16[8,1024,64]{1,2,0:T(8,128)(2,1)S(1)}, f32[8,1024]{1,0:T(8,128)S(1)}, pred[]{:T(512)}, bf16[8,1024,64]{2,1,0:T(8,128)(2,1)}, /*...) while((s32[]{:T(128)}, bf16[8,1024,64]{1,2,0:T(8,128)(2,1)S(1)}, ...), condition=%wide.region_5.6_spmd, body=%wide.region_2.5_spmd.sunk | while | flops 283187200 | bytes 13571689 | solution.py:108
  274.3 51.3 %while.105 = (s32[]{:T(128)}, bf16[8,1024,64]{1,2,0:T(8,128)(2,1)}, f32[8,1024]{1,0:T(8,128)S(1)}, pred[]{:T(512)}, bf16[8,1024,64]{2,1,0:T(8,128)(2,1)}, /*inde...) while((s32[]{:T(128)}, bf16[8,1024,64]{1,2,0:T(8,128)(2,1)}, ...), condition=%wide.region_13.14_spmd, body=%wide.region_10.13_spmd.sunk | while | flops 283187200 | bytes 13571689 | solution.py:108
  331.4 3.5 fusion.210
  337.5 4.5 fusion.216
  342.0 4.2 slice.183
  353.2 5.6 fusion.222
  358.8 4.4 slice.186
  363.9 12.6 %multiply_convert_fusion.3 = (bf16[1024,2048]{1,0:T(8,128)(2,1)}, bf16[1024,2048]{1,0:T(8,128)(2,1)S(1)}, f32[1024,2048]{1,0:T(8,128)}) fusion(f32[2048]{0:T(1024)S(1)} %slice_convert_fusion, f32[1024,2048]{1,0:T(8,128)} %fusion.222, bf16[1024,512]{1,0:T(8,128)(2,1)S(1)} %get-tuple-element.814, bf16[512,2048]{1,0:T(8,128)(2,1)} %slice.183), kind=kOutput, calls=%fused_computation.173 | convolution fusion | flops 2189426688 | bytes 28319744 | tf_op jit(solution)/shard_map/dot_general | solution.py:21
  376.6 6.0 fusion.220
  382.8 5.7 convert_reduce_fusion.4
  388.4 11.7 %convert_reduce_fusion = (f32[2048]{0:T(1024)}, bf16[1024,2048]{1,0:T(8,128)(2,1)S(1)}) fusion(f32[1024,2048]{1,0:T(8,128)} %get-tuple-element.823, f32[2048]{0:T(1024)S(1)} %slice_convert_fusion, bf16[1024,512]{1,0:T(8,128)(2,1)S(1)} %get-tuple-element.800, bf16[2048,512]{1,0:T(8,128)(2,1)S(1)} %copy-done.28), kind=kOutput, calls=%fused_computation.170 | convolution fusion | flops 2195716096 | bytes 15745024 | tf_op jit(solution)/shard_map/dot_general | solution.py:31
  404.5 9.9 convert_reduce_fusion.1
  418.2 4.3 convert_reduce_fusion.6
  432.1 98.4 %while.107 = (s32[]{:T(128)}, bf16[8,1024,64]{1,2,0:T(8,128)(2,1)}, bf16[8,1024,64]{1,2,0:T(8,128)(2,1)}, bf16[8,1024,64]{1,2,0:T(8,128)(2,1)}, pred[]{:T(512)},...) while((s32[]{:T(128)}, bf16[8,1024,64]{1,2,0:T(8,128)(2,1)}, ...), condition=%wide.region_27.28_spmd, body=%wide.region_25.27_spmd.sunk | while | flops 687151104 | bytes 33739384 | solution.py:130
  549.1 4.5 convolution_bitcast_fusion.3
  553.5 4.5 convolution_bitcast_fusion.2
  567.0 112.2 %while.106 = (s32[]{:T(128)}, bf16[8,1024,64]{1,2,0:T(8,128)(2,1)}, bf16[8,1024,64]{1,2,0:T(8,128)(2,1)}, bf16[8,1024,64]{1,2,0:T(8,128)(2,1)}, pred[]{:T(512)},...) while((s32[]{:T(128)}, bf16[8,1024,64]{1,2,0:T(8,128)(2,1)}, ...), condition=%wide.region_20.21_spmd, body=%wide.region_18.20_spmd.sunk | while | flops 687151104 | bytes 33739384 | solution.py:130
  697.1 4.4 convolution_bitcast_fusion
  744.5 5.8 fusion.166
  766.1 10.6 %add.395 = f32[3676160]{0:T(1024)} add(f32[3676160]{0:T(1024)} %constant_dynamic-update-slice_fusion, f32[3676160]{0:T(1024)S(1)} %constant_dynamic-update-slice_fusion.1) | non-fusion elementwise | flops 3676160 | bytes 44113920 | tf_op jit(solution)/shard_map/add | solution.py:323
  780.9 4.1 fusion.189
  786.6 245.9 %all-reduce.7.cloned.1.call-done = f32[3676160]{0:T(1024)} async-done(((f32[3676160]{0:T(1024)}), f32[3676160]{0:T(1024)}) %all-reduce.7.cloned.1.call-update) | async-done | bytes 14704656
  (666 shorter events, 498.7 us)
Async XLA Ops:
  7.2 180.4 %all-reduce.5.cloned.1.call-start = ((), (), s32[]{:S(2)}) async-start(), calls=%async_computation | async-start | bytes 14704640
  16.3 1016.2 %all-reduce.7.cloned.1.call-start = ((), (), s32[]{:S(2)}) async-start(), calls=%async_computation.1 | async-start | bytes 29409280
  19.2 309.2 %copy-start.104 = (f32[1024]{0:T(1024)}, f32[1024]{0:T(1024)S(1)}, u32[]{:S(2)}) copy-start(f32[1024]{0:T(1024)S(1)} %get-tuple-element.831) | copy-start | bytes 12292
  19.2 310.3 %copy-start.106 = (f32[1024]{0:T(1024)}, f32[1024]{0:T(1024)S(1)}, u32[]{:S(2)}) copy-start(f32[1024]{0:T(1024)S(1)} %get-tuple-element.832) | copy-start | bytes 12292
  20.2 309.3 %copy-start.108 = (f32[1024]{0:T(1024)}, f32[1024]{0:T(1024)S(1)}, u32[]{:S(2)}) copy-start(f32[1024]{0:T(1024)S(1)} %add_rsqrt_fusion.3) | copy-start | bytes 12292
  20.2 308.2 %copy-start.110 = (f32[1024]{0:T(1024)}, f32[1024]{0:T(1024)S(1)}, u32[]{:S(2)}) copy-start(f32[1024]{0:T(1024)S(1)} %add_rsqrt_fusion.1) | copy-start | bytes 12292
  194.1 135.4 %copy-start.124 = (f32[512]{0:T(512)}, f32[512]{0:T(512)S(1)}, u32[]{:S(2)}) copy-start(f32[512]{0:T(512)S(1)} %get-tuple-element.788) | copy-start | bytes 6148
  194.1 135.4 %copy-start.128 = (f32[512]{0:T(512)}, f32[512]{0:T(512)S(1)}, u32[]{:S(2)}) copy-start(f32[512]{0:T(512)S(1)} %get-tuple-element.787) | copy-start | bytes 6148
  263.2 64.5 %copy-start.42 = (bf16[512,512]{1,0:T(8,128)(2,1)}, bf16[512,512]{1,0:T(8,128)(2,1)S(1)}, u32[]{:S(2)}) copy-start(bf16[512,512]{1,0:T(8,128)(2,1)S(1)} %slice.175) | copy-start | bytes 1572868
  264.7 64.8 %copy-start.78 = (bf16[512,512]{1,0:T(8,128)(2,1)}, bf16[512,512]{1,0:T(8,128)(2,1)S(1)}, u32[]{:S(2)}) copy-start(bf16[512,512]{1,0:T(8,128)(2,1)S(1)} %slice.165) | copy-start | bytes 1572868
  348.4 15.5 %copy-start.30 = (bf16[1024,512]{1,0:T(8,128)(2,1)}, bf16[1024,512]{1,0:T(8,128)(2,1)S(1)}, u32[]{:S(2)}) copy-start(bf16[1024,512]{1,0:T(8,128)(2,1)S(1)} %get-tuple-element.814) | copy-start | bytes 3145732
  363.9 12.6 %copy-start.28 = (bf16[2048,512]{1,0:T(8,128)(2,1)S(1)}, bf16[2048,512]{1,0:T(8,128)(2,1)}, u32[]{:S(2)}) copy-start(bf16[2048,512]{1,0:T(8,128)(2,1)} %slice.186) | copy-start | bytes 6291460
  388.4 11.8 %copy-start.86 = (bf16[1024,512]{1,0:T(8,128)(2,1)}, bf16[1024,512]{1,0:T(8,128)(2,1)S(1)}, u32[]{:S(2)}) copy-start(bf16[1024,512]{1,0:T(8,128)(2,1)S(1)} %get-tuple-element.800) | copy-start | bytes 3145732
  388.4 14.1 %copy-start.48 = (bf16[1024,512]{1,0:T(8,128)(2,1)}, bf16[1024,512]{1,0:T(8,128)(2,1)S(1)}, u32[]{:S(2)}) copy-start(bf16[1024,512]{1,0:T(8,128)(2,1)S(1)} %get-tuple-element.744) | copy-start | bytes 3145732
  388.4 16.1 %copy-start.88 = (bf16[1024,512]{1,0:T(8,128)(2,1)}, bf16[1024,512]{1,0:T(8,128)(2,1)S(1)}, u32[]{:S(2)}) copy-start(bf16[1024,512]{1,0:T(8,128)(2,1)S(1)} %get-tuple-element.806) | copy-start | bytes 3145732
  388.4 28.4 %copy-start.50 = (bf16[1024,512]{1,0:T(8,128)(2,1)}, bf16[1024,512]{1,0:T(8,128)(2,1)S(1)}, u32[]{:S(2)}) copy-start(bf16[1024,512]{1,0:T(8,128)(2,1)S(1)} %get-tuple-element.809) | copy-start | bytes 3145732
  388.4 11.7 %copy-start.83 = (bf16[512,2048]{1,0:T(8,128)(2,1)S(1)}, bf16[512,2048]{1,0:T(8,128)(2,1)}, u32[]{:S(2)}) copy-start(bf16[512,2048]{1,0:T(8,128)(2,1)} %slice.183) | copy-start | bytes 6291460
  432.1 98.5 %copy-start.38 = (bf16[512,512]{1,0:T(8,128)(2,1)S(1)}, bf16[512,512]{1,0:T(8,128)(2,1)}, u32[]{:S(2)}) copy-start(bf16[512,512]{1,0:T(8,128)(2,1)} %copy-done.37) | copy-start | bytes 1572868
  744.5 12.5 %copy-start.118 = (f32[512]{0:T(512)S(1)}, f32[512]{0:T(512)}, u32[]{:S(2)}) copy-start(f32[512]{0:T(512)} %get-tuple-element.816) | copy-start | bytes 6148
  744.5 13.8 %copy-start.116 = (f32[512]{0:T(512)S(1)}, f32[512]{0:T(512)}, u32[]{:S(2)}) copy-start(f32[512]{0:T(512)} %get-tuple-element.805) | copy-start | bytes 6148
  744.5 15.1 %copy-start.115 = (f32[512]{0:T(512)S(1)}, f32[512]{0:T(512)}, u32[]{:S(2)}) copy-start(f32[512]{0:T(512)} %get-tuple-element.808) | copy-start | bytes 6148
  744.5 16.4 %copy-start.123 = (f32[2048]{0:T(1024)S(1)}, f32[2048]{0:T(1024)}, u32[]{:S(2)}) copy-start(f32[2048]{0:T(1024)} %get-tuple-element.827) | copy-start | bytes 24580
  744.5 17.0 %copy-start.66 = (f32[64,4,8,128]{3,1,2,0:T(4,128)S(1)}, f32[64,4,8,128]{3,1,2,0:T(4,128)}, u32[]{:S(2)}) copy-start(f32[64,4,8,128]{3,1,2,0:T(4,128)} %copy.32) | copy-start | bytes 3145732
  750.4 11.2 %copy-start.67 = (f32[64,4,8,128]{3,1,2,0:T(4,128)S(1)}, f32[64,4,8,128]{3,1,2,0:T(4,128)}, u32[]{:S(2)}) copy-start(f32[64,4,8,128]{3,1,2,0:T(4,128)} %copy.33) | copy-start | bytes 3145732
  (110 other events, 322.8 us)
Sparse Core Ops, SparseCore 0:
  16.4 171.1 all-reduce.4
  776.9 255.5 all-reduce.6
where the time goes:
time: 1050 us; the launch traced here: 1040 us
  matrix products  416 us (40%)
  waiting for transfers between devices  413 us (39%)
  local copies, waits for them, and re-layouts  134 us (13%)
  other arithmetic  60 us (6%)
  between operations  17.1 us (2%)
    unnamed x4, waiting for transfers between devices  413 us
    dot_general x64, matrix products, times_trans(): lax.dot_general(left, right, (((1,), (1,)), ((), ())), preferred_element_...  189 us
    dot_general x48, matrix products, product(): return jnp.dot(left, right, preferred_element_type=jnp.float32)  123 us
    dot_general x48, matrix products, rows_inner(): lax.dot_general(left, right, (((0,), (0,)), ((), ())), preferred_element_...  104 us
    unnamed x315, local copies, waits for them, and re-layouts  74.5 us
  transfers between devices with their start and end apart: 2, of which 2 were waited for; matrix products, arithmetic and copies ran while one was open for 1% of the time, Pallas kernels for 0%

commit v1 on v0

v1 whole, which is shorter than its diff:
```python
import functools
import math

import jax
import jax.numpy as jnp
from jax import lax
from jax.experimental import pallas as pl
from jax.experimental.pallas import tpu as pltpu
from jax.sharding import PartitionSpec as P

D = 512
FF = 2048
HEADS = 8
HD = 64
SHORT = 512
LONG = 1024
PAIR = 2 * HD
PAIRS = HEADS // 2
STRIP = 256

TILE_ROWS = 16
TILE = TILE_ROWS * D

layer_eps = 1e-05
far_below = -1e30

F32 = jnp.float32
BF16 = jnp.bfloat16
MB = 1024 * 1024


def dot_nn(left, right):
    return lax.dot_general(left, right, (((1,), (0,)), ((), ())), preferred_element_type=F32)


def dot_nt(left, right):
    return lax.dot_general(left, right, (((1,), (1,)), ((), ())), preferred_element_type=F32)


def dot_tn(left, right):
    return lax.dot_general(left, right, (((0,), (0,)), ((), ())), preferred_element_type=F32)


def layer_stats(values):
    average = jnp.mean(values, -1, keepdims=True)
    centred = values - average
    variance = jnp.mean(centred * centred, -1, keepdims=True)
    inv_std = lax.rsqrt(variance + layer_eps)
    return (centred * inv_std, inv_std)


def norm_back(grad_hat, normed, inv_std):
    return inv_std * (
        grad_hat
        - jnp.mean(grad_hat, -1, keepdims=True)
        - normed * jnp.mean(grad_hat * normed, -1, keepdims=True)
    )


def sigmoid(values):
    return 0.5 * jnp.tanh(0.5 * values) + 0.5


def fold_rows(values):
    return jnp.sum(values.reshape(values.shape[0] // 8, 8, values.shape[1]), 0)


ROW_QUERY = 0
ROW_KEY = 512
ROW_VALUE = 1024
ROW_OUT = 1536
ROW_GATE_A = 2048
ROW_GATE_F = 2560
ROW_IN = 3072
ROW_DOWN = 5120
ROW_VEC = 7168
ALL_ROWS = 7184


def whole(shape, index=None, single=True):
    rank = len(shape)
    spot = index if index is not None else (0,) * rank
    kwargs = {"pipeline_mode": pl.Buffered(1)} if single else {}
    return pl.BlockSpec(shape, lambda *unused: spot, **kwargs)


PROJ_ROWS = 512


def project_body(tok, w_query, w_key, w_value, vec, hidden, query, key, value):
    normed, unused = layer_stats(tok[...].astype(F32))
    rows = vec[...].astype(F32)
    hid = (normed * rows[0:1] + rows[1:2]).astype(BF16)
    hidden[...] = hid
    query[...] = (dot_nn(hid, w_query[...]) * (1.0 / math.sqrt(HD))).astype(BF16)
    key[...] = dot_nn(hid, w_key[...]).astype(BF16)
    value[...] = dot_nn(hid, w_value[...]).astype(BF16)


def project(tokens, weights):
    total = tokens.shape[0]
    rows = pl.BlockSpec((PROJ_ROWS, D), lambda i: (i, 0))
    square = lambda at: whole((D, D), (at // D, 0))
    shape = jax.ShapeDtypeStruct((total, D), BF16)
    return pl.pallas_call(
        project_body,
        name="project",
        grid=(total // PROJ_ROWS,),
        in_specs=[rows, square(ROW_QUERY), square(ROW_KEY), square(ROW_VALUE), whole((16, D), (ROW_VEC // 16, 0))],
        out_specs=[rows] * 4,
        out_shape=[shape] * 4,
        compiler_params=pltpu.CompilerParams(vmem_limit_bytes=40 * MB),
    )(tokens, weights, weights, weights, weights)


def split_three(values):
    high = values.astype(BF16)
    rest = values - high.astype(F32)
    middle = rest.astype(BF16)
    low = (rest - middle.astype(F32)).astype(BF16)
    return high, middle, low


def pick_lanes(base, lane, first, columns):
    out = base
    for offset, column in enumerate(columns):
        out = jnp.where(lane == first + offset, column, out)
    return out


def attend_body(long_ref, query, key, value, attended, extra):
    sub = pl.program_id(0)
    is_long = long_ref[sub] > 0
    lane = lax.broadcasted_iota(jnp.int32, (STRIP, PAIR), 1)
    row_ids = lax.broadcasted_iota(jnp.int32, (STRIP, STRIP), 0)
    col_ids = lax.broadcasted_iota(jnp.int32, (STRIP, STRIP), 1)
    causal = row_ids >= col_ids
    cut = jnp.where(is_long, 0.0, far_below)
    keys = key[...]
    values = value[...]
    for strip in range(LONG // STRIP):
        rows = pl.ds(strip * STRIP, STRIP)
        reach = (strip + 1) * STRIP
        q_rows = query[rows, :]
        far = strip * STRIP >= SHORT
        tail = jnp.zeros((STRIP, PAIR), F32)
        outs = []
        for head in range(2):
            mine = (lane < HD) if head == 0 else (lane >= HD)
            q_head = jnp.where(mine, q_rows, jnp.zeros_like(q_rows))
            scores = dot_nt(q_head, keys[:reach])
            parts = []
            if far:
                parts.append(scores[:, :SHORT] + cut)
                if reach - STRIP > SHORT:
                    parts.append(scores[:, SHORT : reach - STRIP])
            elif strip:
                parts.append(scores[:, : reach - STRIP])
            parts.append(jnp.where(causal, scores[:, reach - STRIP :], far_below))
            scores = jnp.concatenate(parts, 1)
            largest = jnp.max(scores, -1, keepdims=True)
            shifted = jnp.exp(scores - largest)
            sum_exp = jnp.sum(shifted, -1, keepdims=True)
            out = dot_nn(shifted.astype(BF16), values[:reach]) * (1.0 / sum_exp)
            outs.append(out)
            high, middle, low = split_three(-(largest + jnp.log(sum_exp)))
            tail = pick_lanes(tail, lane, 3 * head, [t.astype(F32) for t in (high, middle, low)])
        if far:
            tail = jnp.where(lane == 6, jnp.where(is_long, 0.0, 1.0), tail)
        attended[rows, :] = jnp.where(lane < HD, outs[0], outs[1]).astype(BF16)
        extra[rows, :] = tail.astype(BF16)


def attend(longs, query, key, value):
    total = query.shape[0]
    block = pl.BlockSpec((LONG, PAIR), lambda s, p, l: (s, p))
    shape = jax.ShapeDtypeStruct((total, D), BF16)
    return pl.pallas_call(
        attend_body,
        name="attend",
        grid_spec=pltpu.PrefetchScalarGridSpec(
            num_scalar_prefetch=1,
            grid=(total // LONG, PAIRS),
            in_specs=[block] * 3,
            out_specs=[block] * 2,
        ),
        out_shape=[shape] * 2,
        compiler_params=pltpu.CompilerParams(vmem_limit_bytes=40 * MB),
    )(longs, query, key, value)


def attend_back_body(long_ref, query, key, value, extra, attended, grad, grad_query, grad_key, grad_value):
    lane = lax.broadcasted_iota(jnp.int32, (LONG, PAIR), 1)
    row = lax.broadcasted_iota(jnp.int32, (LONG, PAIR), 0)
    row_ids = lax.broadcasted_iota(jnp.int32, (STRIP, STRIP), 0)
    col_ids = lax.broadcasted_iota(jnp.int32, (STRIP, STRIP), 1)
    causal = col_ids >= row_ids
    q_all, k_all, v_all, g_all, x_all = query[...], key[...], value[...], grad[...], extra[...]
    product = g_all.astype(F32) * attended[...].astype(F32)
    zero = jnp.zeros_like(q_all)
    early = jnp.where((lane == 6) & (row < SHORT), far_below, 0.0)
    v_tail = jnp.where(lane < 3, 1.0, 0.0).astype(BF16)
    v_wide = jnp.concatenate([v_all, v_tail], 1)
    heads = []
    for head in range(2):
        mine = (lane < HD) if head == 0 else (lane >= HD)
        delta = jnp.sum(jnp.where(mine, product, 0.0), -1, keepdims=True)
        d_tail = pick_lanes(jnp.zeros((LONG, PAIR), F32), lane, 0, [t.astype(F32) for t in split_three(-delta)])
        q_head = jnp.where(mine, q_all, zero)
        g_head = jnp.where(mine, g_all, zero)
        k_head = jnp.where(mine, k_all, zero)
        ones = jnp.where((lane >= 3 * head) & (lane < 3 * head + 3), 1.0, early).astype(BF16)
        heads.append(
            (
                q_head,
                g_head,
                k_head,
                jnp.concatenate([q_head, x_all], 1),
                jnp.concatenate([g_head, d_tail.astype(BF16)], 1),
                jnp.concatenate([k_all, ones], 1),
            )
        )
    blocks = LONG // STRIP
    query_sum = [jnp.zeros((STRIP, PAIR), F32) for unused in range(blocks)]
    for block in range(blocks):
        lo, hi = block * STRIP, (block + 1) * STRIP
        key_sum = jnp.zeros((STRIP, PAIR), F32)
        value_sum = jnp.zeros((STRIP, PAIR), F32)
        for q_head, g_head, k_head, q_wide, g_wide, k_wide in heads:
            soft = jnp.exp(dot_nt(k_wide[lo:hi], q_wide[lo:]))
            first = jnp.where(causal, soft[:, :STRIP], 0.0)
            soft = first if hi == LONG else jnp.concatenate([first, soft[:, STRIP:]], 1)
            slope = dot_nt(v_wide[lo:hi], g_wide[lo:])
            scores = (soft * slope).astype(BF16)
            value_sum += dot_nn(soft.astype(BF16), g_head[lo:])
            key_sum += dot_nn(scores, q_head[lo:])
            part = dot_tn(scores, k_head[lo:hi])
            for later in range(block, blocks):
                query_sum[later] += part[(later - block) * STRIP : (later - block + 1) * STRIP]
        grad_key[lo:hi, :] = key_sum.astype(BF16)
        grad_value[lo:hi, :] = value_sum.astype(BF16)
        grad_query[lo:hi, :] = (query_sum[block] * (1.0 / math.sqrt(HD))).astype(BF16)


def attend_back(longs, query, key, value, extra, attended, grad):
    total = query.shape[0]
    block = pl.BlockSpec((LONG, PAIR), lambda s, p, l: (s, p))
    shape = jax.ShapeDtypeStruct((total, D), BF16)
    return pl.pallas_call(
        attend_back_body,
        name="attend_back",
        grid_spec=pltpu.PrefetchScalarGridSpec(
            num_scalar_prefetch=1,
            grid=(total // LONG, PAIRS),
            in_specs=[block] * 6,
            out_specs=[block] * 3,
        ),
        out_shape=[shape] * 3,
        compiler_params=pltpu.CompilerParams(vmem_limit_bytes=48 * MB),
    )(longs, query, key, value, extra, attended, grad)


MID_ROWS = 256
CHUNKS = FF // D
TANH_SCALE = math.sqrt(2.0 / math.pi)


def spread_matrix(size):
    quarter = size // CHUNKS
    to = lax.broadcasted_iota(jnp.int32, (size, size), 0)
    source = lax.broadcasted_iota(jnp.int32, (size, size), 1)
    return (source == CHUNKS * (to % quarter) + to // quarter).astype(BF16)


def middle_body(
    steps,
    tok,
    grad_out,
    hidden_a,
    attended,
    w_out,
    gate_attn,
    gate_ffn,
    w_in,
    w_down,
    vec,
    outputs,
    grad_middle_ref,
    grad_za_ref,
    grad_attended,
    d_out,
    d_gate_a,
    d_gate_f,
    d_in,
    d_down,
    d_vec,
    wide,
    slope,
    s_active,
    s_grad_pre,
    s_hidden_f,
    s_grad_f,
    s_grad_zf,
    s_grad_a,
    s_grad_za,
    s_hidden_a,
    s_attended,
    s_vec,
):
    step = pl.program_id(0)

    @pl.when(step == 0)
    def _():
        shuffle = spread_matrix(256)
        for block in range(FF // 256):
            part = dot_nn(shuffle, w_in[block * 256 : (block + 1) * 256, :]).astype(BF16)
            for chunk in range(CHUNKS):
                wide[chunk, block * 64 : (block + 1) * 64, :] = part[chunk * 64 : (chunk + 1) * 64]
        s_vec[...] = jnp.zeros_like(s_vec)

    here = pl.ds(pl.multiple_of(step * MID_ROWS, MID_ROWS), MID_ROWS)
    vecs = vec[...].astype(F32)
    hid_a = hidden_a[...]
    att = attended[...]
    grad = grad_out[...].astype(F32)
    branch_a = dot_nn(att, w_out[...]) + vecs[2:3]
    gate_a = sigmoid(dot_nn(hid_a, gate_attn[...]) + vecs[3:4])
    middle = tok[...].astype(F32) + gate_a * branch_a
    normed, inv_std = layer_stats(middle)
    hid_f = (normed * vecs[4:5] + vecs[5:6]).astype(BF16)
    s_hidden_f[here, :] = hid_f
    s_hidden_a[here, :] = hid_a
    s_attended[here, :] = att
    gate_f = sigmoid(dot_nn(hid_f, gate_ffn[...]) + vecs[7:8])
    branch_f = jnp.zeros((MID_ROWS, D), F32) + vecs[6:7]
    for chunk in range(CHUNKS):
        cols = slice(chunk * D, (chunk + 1) * D)
        pre = dot_nn(hid_f, wide[chunk]) + vecs[8 + chunk : 9 + chunk]
        square = pre * pre
        bend = jnp.tanh(pre * (TANH_SCALE + (TANH_SCALE * 0.044715) * square))
        half = 0.5 * (1.0 + bend)
        active = (pre * half).astype(BF16)
        slope[:, cols] = half + (0.5 * pre) * (1.0 - bend * bend) * (
            TANH_SCALE + (3.0 * 0.044715 * TANH_SCALE) * square
        )
        s_active[here, cols] = active
        branch_f += dot_nn(active, w_down[chunk * D : (chunk + 1) * D, :])
    outputs[...] = (middle + gate_f * branch_f).astype(BF16)

    grad_branch_f = (grad * gate_f).astype(BF16)
    grad_zf = (grad * branch_f * gate_f * (1.0 - gate_f)).astype(BF16)
    s_grad_f[here, :] = grad_branch_f
    s_grad_zf[here, :] = grad_zf
    s_vec[6] += fold_rows(grad_branch_f.astype(F32))
    s_vec[7] += fold_rows(grad_zf.astype(F32))
    grad_hidden = dot_nt(grad_zf, gate_ffn[...])
    for chunk in range(CHUNKS):
        cols = slice(chunk * D, (chunk + 1) * D)
        grad_active = dot_nt(grad_branch_f, w_down[chunk * D : (chunk + 1) * D, :])
        grad_pre = (grad_active * slope[:, cols]).astype(BF16)
        s_grad_pre[here, cols] = grad_pre
        s_vec[8 + chunk] += fold_rows(grad_pre.astype(F32))
        grad_hidden += dot_nt(grad_pre, wide[chunk])
    s_vec[4] += fold_rows(grad_hidden * normed)
    s_vec[5] += fold_rows(grad_hidden)
    grad_middle = grad + norm_back(grad_hidden * vecs[4:5], normed, inv_std)
    grad_middle_ref[...] = grad_middle
    grad_branch_a = (grad_middle * gate_a).astype(BF16)
    grad_za = (grad_middle * branch_a * gate_a * (1.0 - gate_a)).astype(BF16)
    grad_za_ref[...] = grad_za
    s_grad_a[here, :] = grad_branch_a
    s_grad_za[here, :] = grad_za
    s_vec[2] += fold_rows(grad_branch_a.astype(F32))
    s_vec[3] += fold_rows(grad_za.astype(F32))
    grad_attended[...] = dot_nt(grad_branch_a, w_out[...]).astype(BF16)

    @pl.when(step == steps - 1)
    def _():
        for chunk in range(CHUNKS):
            cols = slice(chunk * D, (chunk + 1) * D)
            d_down[cols, :] = dot_tn(s_active[:, cols], s_grad_f[...]).astype(BF16)
            wide[chunk] = dot_tn(s_hidden_f[...], s_grad_pre[:, cols]).astype(BF16)
        shuffle = spread_matrix(256)
        for block in range(FF // 256):
            parts = [wide[chunk, block * 64 : (block + 1) * 64, :] for chunk in range(CHUNKS)]
            d_in[block * 256 : (block + 1) * 256, :] = dot_tn(shuffle, jnp.concatenate(parts, 0)).astype(BF16)
        d_out[...] = dot_tn(s_attended[...], s_grad_a[...]).astype(BF16)
        d_gate_a[...] = dot_tn(s_hidden_a[...], s_grad_za[...]).astype(BF16)
        d_gate_f[...] = dot_tn(s_hidden_f[...], s_grad_zf[...]).astype(BF16)
        d_vec[...] = jnp.sum(s_vec[...], 1)


def middle_part(tokens, grad_out, hidden_a, attended, weights):
    total = tokens.shape[0]
    steps = total // MID_ROWS
    rows = pl.BlockSpec((MID_ROWS, D), lambda i: (i, 0))
    square = lambda at: whole((D, D), (at // D, 0))
    rows_of = lambda kind: jax.ShapeDtypeStruct((total, D), kind)
    kept = lambda count: pltpu.VMEM((total, count), BF16)
    fixed = lambda count, kind: jax.ShapeDtypeStruct((count, D), kind)
    return pl.pallas_call(
        functools.partial(middle_body, steps),
        name="middle_part",
        grid=(steps,),
        in_specs=[rows] * 4
        + [square(ROW_OUT), square(ROW_GATE_A), square(ROW_GATE_F)]
        + [
            pl.BlockSpec((pl.Element(FF), pl.Element(D)), lambda i: (ROW_IN, 0), pipeline_mode=pl.Buffered(1)),
            pl.BlockSpec((pl.Element(FF), pl.Element(D)), lambda i: (ROW_DOWN, 0), pipeline_mode=pl.Buffered(1)),
            whole((16, D), (ROW_VEC // 16, 0)),
        ],
        out_specs=[rows] * 4
        + [whole((D, D))] * 3
        + [whole((FF, D))] * 2
        + [whole((16, D))],
        out_shape=[rows_of(BF16), rows_of(F32), rows_of(BF16), rows_of(BF16)]
        + [fixed(D, BF16)] * 3
        + [fixed(FF, BF16)] * 2
        + [fixed(16, F32)],
        scratch_shapes=[
            pltpu.VMEM((CHUNKS, D, D), BF16),
            pltpu.VMEM((MID_ROWS, FF), F32),
            kept(FF),
            kept(FF),
            kept(D),
            kept(D),
            kept(D),
            kept(D),
            kept(D),
            kept(D),
            kept(D),
            pltpu.VMEM((16, 8, D), F32),
        ],
        compiler_params=pltpu.CompilerParams(vmem_limit_bytes=62 * MB),
    )(tokens, grad_out, hidden_a, attended, *([weights] * 6))


LAST_ROWS = 512


def last_body(
    steps,
    tok,
    grad_middle,
    grad_za,
    hidden_a,
    grad_query,
    grad_key,
    grad_value,
    w_query,
    w_key,
    w_value,
    gate_attn,
    vec,
    input_grad,
    d_query,
    d_key,
    d_value,
    d_vec,
    s_vec,
):
    step = pl.program_id(0)

    @pl.when(step == 0)
    def _():
        s_vec[...] = jnp.zeros_like(s_vec)

    here = pl.ds(pl.multiple_of(step * LAST_ROWS, LAST_ROWS), LAST_ROWS)
    vecs = vec[...].astype(F32)
    normed, inv_std = layer_stats(tok[...].astype(F32))
    grad_hidden = (
        dot_nt(grad_query[here, :], w_query[...])
        + dot_nt(grad_key[here, :], w_key[...])
        + dot_nt(grad_value[here, :], w_value[...])
        + dot_nt(grad_za[...], gate_attn[...])
    )
    s_vec[0] += fold_rows(grad_hidden * normed)
    s_vec[1] += fold_rows(grad_hidden)
    input_grad[...] = (grad_middle[...] + norm_back(grad_hidden * vecs[0:1], normed, inv_std)).astype(BF16)

    @pl.when(step == steps - 1)
    def _():
        d_query[...] = dot_tn(hidden_a[...], grad_query[...]).astype(BF16)
        d_key[...] = dot_tn(hidden_a[...], grad_key[...]).astype(BF16)
        d_value[...] = dot_tn(hidden_a[...], grad_value[...]).astype(BF16)
        d_vec[...] = jnp.sum(s_vec[...], 1)


def last_part(tokens, grad_middle, grad_za, hidden_a, grad_query, grad_key, grad_value, weights):
    total = tokens.shape[0]
    steps = total // LAST_ROWS
    rows = pl.BlockSpec((LAST_ROWS, D), lambda i: (i, 0))
    square = lambda at: whole((D, D), (at // D, 0))
    full = whole((total, D))
    fixed = jax.ShapeDtypeStruct((D, D), BF16)
    return pl.pallas_call(
        functools.partial(last_body, steps),
        name="last_part",
        grid=(steps,),
        in_specs=[rows] * 3
        + [full] * 4
        + [square(ROW_QUERY), square(ROW_KEY), square(ROW_VALUE), square(ROW_GATE_A), whole((16, D), (ROW_VEC // 16, 0))],
        out_specs=[rows] + [whole((D, D))] * 3 + [whole((16, D))],
        out_shape=[jax.ShapeDtypeStruct((total, D), BF16)] + [fixed] * 3 + [jax.ShapeDtypeStruct((16, D), F32)],
        scratch_shapes=[pltpu.VMEM((16, 8, D), F32)],
        compiler_params=pltpu.CompilerParams(vmem_limit_bytes=48 * MB),
    )(tokens, grad_middle, grad_za, hidden_a, grad_query, grad_key, grad_value, *([weights] * 5))


def local_part(weights, tokens, out_grad, longs):
    subs, length, unused = tokens.shape
    rows = tokens.reshape(subs * length, D)
    grads = out_grad.reshape(subs * length, D)
    hidden_a, query, key, value = project(rows, weights)
    attended, extra = attend(longs, query, key, value)
    (outputs, grad_middle, grad_za, grad_attended, d_out, d_gate_a, d_gate_f, d_in, d_down, vec_one) = middle_part(
        rows, grads, hidden_a, attended, weights
    )
    grad_query, grad_key, grad_value = attend_back(longs, query, key, value, extra, attended, grad_attended)
    input_grad, d_query, d_key, d_value, vec_two = last_part(
        rows, grad_middle, grad_za, hidden_a, grad_query, grad_key, grad_value, weights
    )
    gradient = jnp.concatenate(
        [d_query, d_key, d_value, d_out, d_gate_a, d_gate_f, d_in, d_down, (vec_one + vec_two).astype(BF16)], 0
    )
    return outputs.reshape(tokens.shape), input_grad.reshape(tokens.shape), gradient


def share_tiles(share, count):
    starts = [index * share // TILE for index in range(count)]
    ends = [-(-((index + 1) * share) // TILE) for index in range(count)]
    return starts, max(end - start for start, end in zip(starts, ends))


def assemble(blocks, starts):
    count, rows, unused = blocks.shape
    pieces = []
    for index in range(count):
        lo = starts[index] * TILE_ROWS
        hi = (starts[index + 1] if index + 1 < count else ALL_ROWS // TILE_ROWS) * TILE_ROWS
        piece = blocks[index, : hi - lo]
        if index and (starts[index - 1] * TILE_ROWS + rows) > lo:
            over = starts[index - 1] * TILE_ROWS + rows - lo
            before = blocks[index - 1, rows - over :]
            piece = jnp.concatenate([piece[:over] + before, piece[over:]], 0)
        pieces.append(piece)
    return jnp.concatenate(pieces, 0)


def on_device(axes, sizes, tokens, out_grad, long_count, params):
    count = math.prod(sizes)
    share = params.shape[0]
    starts, tiles = share_tiles(share, count)
    rows = tiles * TILE_ROWS
    me = lax.axis_index(axes)
    offset = (me * share) % TILE
    padded = lax.dynamic_update_slice(jnp.zeros((rows * D,), F32), params, (offset,))
    block = padded.reshape(rows, D).astype(BF16)
    gathered = lax.all_gather(block, axes, axis=0, tiled=False)
    weights = assemble(gathered, starts)
    outputs, input_grad, gradient = local_part(weights, tokens, out_grad, long_count.reshape(-1))
    limit = gradient.shape[0]
    spread = []
    for index in range(count):
        lo = starts[index] * TILE_ROWS
        piece = gradient[lo : min(lo + rows, limit)]
        if lo + rows > limit:
            piece = jnp.pad(piece, ((0, lo + rows - limit), (0, 0)))
        spread.append(piece)
    summed = lax.psum_scatter(jnp.stack(spread), axes, scatter_dimension=0, tiled=False)
    param_grad = lax.dynamic_slice(summed.astype(F32).reshape(-1), (offset,), (share,))
    return (outputs, input_grad, param_grad)


def solution(mesh):
    axes = ("wide", "narrow")
    sizes = tuple(mesh.shape[axis] for axis in axes)
    return jax.shard_map(
        functools.partial(on_device, axes, sizes),
        mesh=mesh,
        in_specs=(
            P(None, axes, None),
            P(None, axes, None),
            P(None, axes),
            P(axes),
        ),
        out_specs=(
            P(None, axes, None),
            P(None, axes, None),
            P(axes),
        ),
        check_vma=False,
    )
```

time: 1050 us -> 463 us (0.44)
  matrix products: 416 us -> 0 us
  waiting for transfers between devices: 413 us -> 199 us
  Pallas kernels: 0 us -> 148 us
  local copies, waits for them, and re-layouts: 134 us -> 65.2 us
  other arithmetic: 60 us -> 29.8 us
    dot_general x160 -> x0, matrix products: 416 us -> none  [the longest x64 189 us: times_trans(): lax.dot_general(left, right, (((1,), (1,)), ((), ())), preferred_element_...]
    unnamed x4 -> x2, waiting for transfers between devices: 413 us -> 0.03 us
    pallas_call x0 -> x5, Pallas kernels: none -> 148 us  [the longest x1 58.6 us: middle_part(): pl.pallas_call(functools.partial(middle_body, steps), name='middle_part',...]
    reduce_scatter x0 -> x1, waiting for transfers between devices: none -> 121 us  [on_device(): lax.psum_scatter(jnp.stack(spread), axes, scatter_dimension=0, tiled=False)]
    all_gather x0 -> x1, waiting for transfers between devices: none -> 78.2 us  [on_device(): gathered = lax.all_gather(block, axes, axis=0, tiled=False)]
    unnamed x0 -> x39, other arithmetic: none -> 29.1 us
    convert_element_type x20 -> x1, other arithmetic: 23.4 us -> 0.01 us  [local_part(): (vec_one + vec_two).astype(BF16)]
    slice x11 -> x0, local copies, waits for them, and re-layouts: 23.2 us -> none  [the longest x7 9.59 us: unpack(): buffer[position * square:(position + 1) * square].reshape(D, D)]
  transfers between devices with their start and end apart: 2 -> 2, of which waited for: 2 -> 2; matrix products, arithmetic and copies ran while one was open for 1% -> 0% of each run, Pallas kernels for 0% -> 0%
where the time goes in v1:
time: 463 us; the launch traced here: 457 us
  waiting for transfers between devices  199 us (43%)
  Pallas kernels  148 us (32%)
  local copies, waits for them, and re-layouts  65.2 us (14%)
  other arithmetic  29.8 us (6%)
  between operations  14.3 us (3%)
    reduce_scatter x1, waiting for transfers between devices, on_device(): lax.psum_scatter(jnp.stack(spread), axes, scatter_dimension=0, tiled=False)  121 us
    all_gather x1, waiting for transfers between devices, on_device(): gathered = lax.all_gather(block, axes, axis=0, tiled=False)  78.2 us
    pallas_call x1, Pallas kernels, middle_part(): pl.pallas_call(functools.partial(middle_body, steps), name='middle_part',...  58.6 us
    unnamed x94, local copies, waits for them, and re-layouts  57.9 us
    pallas_call x1, Pallas kernels, attend_back(): pl.pallas_call(attend_back_body, name='attend_back', grid_spec=pltpu.Pref...  36.8 us
    pallas_call x1, Pallas kernels, attend(): pl.pallas_call(attend_body, name='attend', grid_spec=pltpu.PrefetchScalar...  30.8 us
    unnamed x39, other arithmetic  29.1 us
    pallas_call x1, Pallas kernels, last_part(): pl.pallas_call(functools.partial(last_body, steps), name='last_part', gri...  15.5 us
  transfers between devices with their start and end apart: 2, of which 2 were waited for; matrix products, arithmetic and copies ran while one was open for 0% of the time, Pallas kernels for 0%

profile of v1, /device:TPU:0, one launch (start us, length us, event | category | flops | bytes accessed | tf_op | source)
XLA Modules:
  0.0 457.0 jit_solution(14833490643046984426)
XLA Ops:
  7.3 4.5 dynamic_update_slice.3
  12.7 78.2 %all-gather.2.cloned.1.call-done = bf16[32,240,512]{2,1,0:T(8,128)(2,1)} async-done(((bf16[1,240,512]{2,1,0:T(8,128)(2,1)}), bf16[32,240,512]{2,1,0:T(8,128)(2,1)}) %all-gather.2.cloned.1.call-update) | async-done | bytes 7864336 | tf_op jit(solution)/shard_map/all_gather | solution.py:559
  90.9 1.0 fusion.17
  92.7 1.1 fusion.47
  94.5 0.9 fusion.46
  96.2 0.9 fusion.45
  97.9 0.9 fusion.44
  99.6 0.9 fusion.43
  143.6 1.0 fusion.16.w_query.w_key.w_value.vec.w_out.gate_attn.gate_ffn.w_in.w_down
  144.6 2.9 copy-done.12
  147.5 6.5 %project.1 = (bf16[2048,512]{1,0:T(8,128)(2,1)S(1)}, bf16[2048,512]{1,0:T(8,128)(2,1)S(1)}, bf16[2048,512]{1,0:T(8,128)(2,1)S(1)}, bf16[2048,512]{1,0:T(8,128)(2,1)S(1)}) custom-call(bf16[2048,512]{1,0:T(8,128)(2,1)S(1)} %bitcast.341, bf16[7184,512]{1,0:T(8,128)(2,1)} %copy-done.12, bf16[7184,512]{1,0:T(8,128)(2,1)} %copy-done.12, ...), custom_call_target="tpu_custom_call" | custom-call | tf_op jit(solution)/shard_map/project/pallas_call | solution.py:105
  154.1 1.3 copy-done.2
  155.4 30.8 %attend.1 = (bf16[2048,512]{1,0:T(8,128)(2,1)S(1)}, bf16[2048,512]{1,0:T(8,128)(2,1)S(1)}) custom-call(s32[2]{0:T(128)S(1)} %bitcast.343, bf16[2048,512]{1,0:T(8,128)(2,1)S(1)} %get-tuple-element.28.query, bf16[2048,512]{1,0:T(8,128)(2,1)S(1)} %get-tuple-element.29.key, bf16[2048,512]{1,0:T(8,128)(2,1)S(1)} %get-tuple-element.30.value), custom_call_target="tpu_custom_call" | custom-call | tf_op jit(solution)/shard_map/attend/pallas_call | solution.py:178
  186.2 1.3 copy-done.3
  187.5 1.3 copy-done.6
  188.9 1.4 copy-done.8
  190.3 58.6 %middle_part.1 = (bf16[2048,512]{1,0:T(8,128)(2,1)}, f32[2048,512]{1,0:T(8,128)}, bf16[2048,512]{1,0:T(8,128)(2,1)}, bf16[2048,512]{1,0:T(8,128)(2,1)}, bf16[512...) custom-call(bf16[2048,512]{1,0:T(8,128)(2,1)} %bitcast.340, ...), custom_call_target="tpu_custom_call" | custom-call | tf_op jit(solution)/shard_map/middle_part/pallas_call | solution.py:401
  248.9 36.8 %attend_back.1 = (bf16[2048,512]{1,0:T(8,128)(2,1)S(1)}, bf16[2048,512]{1,0:T(8,128)(2,1)S(1)}, bf16[2048,512]{1,0:T(8,128)(2,1)}) custom-call(s32[2]{0:T(128)S(1)} %bitcast.344, bf16[2048,512]{1,0:T(8,128)(2,1)} %copy-done.3, bf16[2048,512]{1,0:T(8,128)(2,1)} %copy-done.4, bf16[2048,512]{1,0:T(8,128)(2,1)} %copy-done.5, bf16[2048,512]{1,0:T(8,128)(2,1)} %copy-done.8, ...), custom_call_target="tpu_custom_call" | custom-call | tf_op jit(solution)/shard_map/attend_back/pallas_call | solution.py:249
  285.7 1.4 copy-done.9
  287.1 1.3 copy-done.10
  288.4 15.5 %last_part.1 = (bf16[2048,512]{1,0:T(8,128)(2,1)}, bf16[512,512]{1,0:T(8,128)(2,1)S(1)}, bf16[512,512]{1,0:T(8,128)(2,1)S(1)}, bf16[512,512]{1,0:T(8,128)(2,1)S(1)}, f32[16,512]{1,0:T(8,128)S(1)}) custom-call(bf16[2048,512]{1,0:T(8,128)(2,1)S(1)} %bitcast.342, f32[2048,512]{1,0:T(8,128)} %get-tuple-element.33.grad_middle, bf16[2048,512]{1,0:T(8,128)(2,1)S(1)} %copy-done.7, ...), custom_call_target="tpu_custom_call" | custom-call | tf_op jit(solution)/shard_map/last_part/pallas_call | solution.py:496
  326.9 121.2 %reduce-scatter.2.cloned.1.call-done = bf16[1,240,512]{2,1,0:T(8,128)(2,1)} async-done(((bf16[32,240,512]{2,1,0:T(8,128)(2,1)}), bf16[1,240,512]{2,1,0:T(8,128)(2,1)}) %reduce-scatter.2.cloned.1.call-update) | async-done | bytes 245776 | tf_op jit(solution)/shard_map/reduce_scatter | solution.py:570
  448.1 1.0 convert_bitcast_fusion
  449.2 1.0 dynamic_slice.3
  (127 shorter events, 70.8 us)
Async XLA Ops:
  7.2 83.8 %all-gather.2.cloned.1.call-start = ((), (), s32[]{:S(2)}) async-start(), calls=%async_computation.1 | async-start | bytes 8110080 | tf_op jit(solution)/shard_map/all_gather | solution.py:559
  12.7 435.4 %reduce-scatter.2.cloned.1.call-start = ((), (), s32[]{:S(2)}) async-start(), calls=%async_computation.2 | async-start | bytes 8110080 | tf_op jit(solution)/shard_map/reduce_scatter | solution.py:570
  92.6 54.9 %copy-start = (bf16[2,1024,512]{2,1,0:T(8,128)(2,1)S(1)}, bf16[2,1024,512]{2,1,0:T(8,128)(2,1)}, u32[]{:S(2)}) copy-start(bf16[2,1024,512]{2,1,0:T(8,128)(2,1)} %param.4) | copy-start | bytes 6291460
  144.6 2.9 copy-start.12
  147.5 7.9 %copy-start.11 = (s32[2,1]{0,1:T(1,128)S(1)}, s32[2,1]{0,1:T(1,128)}, u32[]{:S(2)}) copy-start(s32[2,1]{0,1:T(1,128)} %param.6) | copy-start | bytes 28
  154.1 1.3 copy-start.2
  155.4 30.8 %copy-start.4 = (bf16[2048,512]{1,0:T(8,128)(2,1)}, bf16[2048,512]{1,0:T(8,128)(2,1)S(1)}, u32[]{:S(2)}) copy-start(bf16[2048,512]{1,0:T(8,128)(2,1)S(1)} %get-tuple-element.29.key) | copy-start | bytes 6291460
  155.4 34.9 %copy-start.5 = (bf16[2048,512]{1,0:T(8,128)(2,1)}, bf16[2048,512]{1,0:T(8,128)(2,1)S(1)}, u32[]{:S(2)}) copy-start(bf16[2048,512]{1,0:T(8,128)(2,1)S(1)} %get-tuple-element.30.value) | copy-start | bytes 6291460
  186.2 1.3 copy-start.3
  187.5 1.3 copy-start.6
  188.9 1.4 copy-start.8
  248.8 39.6 %copy-start.1 = (bf16[2,1024,512]{2,1,0:T(8,128)(2,1)S(1)}, bf16[2,1024,512]{2,1,0:T(8,128)(2,1)}, u32[]{:S(2)}) copy-start(bf16[2,1024,512]{2,1,0:T(8,128)(2,1)} %param.4) | copy-start | bytes 6291460
  248.9 39.5 %copy-start.7 = (bf16[2048,512]{1,0:T(8,128)(2,1)S(1)}, bf16[2048,512]{1,0:T(8,128)(2,1)}, u32[]{:S(2)}) copy-start(bf16[2048,512]{1,0:T(8,128)(2,1)} %get-tuple-element.34.grad_za) | copy-start | bytes 6291460
  285.7 1.4 copy-start.9
  287.1 1.3 copy-start.10
  288.4 19.8 %copy-start.15 = (bf16[512,512]{1,0:T(8,128)(2,1)S(1)}, bf16[512,512]{1,0:T(8,128)(2,1)}, u32[]{:S(2)}) copy-start(bf16[512,512]{1,0:T(8,128)(2,1)} %get-tuple-element.44) | copy-start | bytes 1572868
  288.4 21.9 %copy-start.16 = (bf16[512,512]{1,0:T(8,128)(2,1)S(1)}, bf16[512,512]{1,0:T(8,128)(2,1)}, u32[]{:S(2)}) copy-start(bf16[512,512]{1,0:T(8,128)(2,1)} %get-tuple-element.45) | copy-start | bytes 1572868
  303.9 7.9 %copy-start.17 = (bf16[512,512]{1,0:T(8,128)(2,1)S(1)}, bf16[512,512]{1,0:T(8,128)(2,1)}, u32[]{:S(2)}) copy-start(bf16[512,512]{1,0:T(8,128)(2,1)} %get-tuple-element.46) | copy-start | bytes 1572868
  303.9 9.3 %copy-start.14 = (bf16[2048,512]{1,0:T(8,128)(2,1)S(1)}, bf16[2048,512]{1,0:T(8,128)(2,1)}, u32[]{:S(2)}) copy-start(bf16[2048,512]{1,0:T(8,128)(2,1)} %get-tuple-element.47) | copy-start | bytes 6291460
  306.1 13.7 %copy-start.13 = (bf16[2048,512]{1,0:T(8,128)(2,1)S(1)}, bf16[2048,512]{1,0:T(8,128)(2,1)}, u32[]{:S(2)}) copy-start(bf16[2048,512]{1,0:T(8,128)(2,1)} %get-tuple-element.48) | copy-start | bytes 6291460
  313.2 12.9 %copy-start.18 = (f32[16,512]{1,0:T(8,128)S(1)}, f32[16,512]{1,0:T(8,128)}, u32[]{:S(2)}) copy-start(f32[16,512]{1,0:T(8,128)} %get-tuple-element.49) | copy-start | bytes 98308
Sparse Core Ops, SparseCore 0:
  12.8 78.0 all-gather.1
  327.0 120.9 reduce-scatter.1
